TPU v7x, 32 devices: a whole 2x2x4 slice. The times are simulated.
32 devices in a mesh: seq: 8 (over y, x, core), ch: 4 (over z).
Axes of the slice: x: 2, y: 2, z: 4, core: 2. Of those that a mesh axis runs over, the one named last changes fastest.
Arguments:
- inputs: bfloat16 [32, 2048, 768], P(None, 'seq'), may hold values from -6 to 6
- lengths: int32 [32], replicated, may hold values from 256 to 1024, as said below
- input_gain: float32 [768], replicated, may hold values from 0.25 to 1.75
- input_shift: float32 [768], replicated, may hold values from -3 to 3
- conv_weight: bfloat16 [5, 768, 768], replicated, may hold values from -0.09375 to 0.09375
- branch_gain: float32 [768], P('ch'), may hold values from 0.25 to 1.75
- branch_shift: float32 [768], P('ch'), may hold values from -3 to 3
- dilated_tap_weight: bfloat16 [3, 768, 384], P(None, None, 'ch'), may hold values from -0.125 to 0.125
- mixer_gain: float32 [384], P('ch'), may hold values from 0.25 to 1.75
- mixer_shift: float32 [384], P('ch'), may hold values from -3 to 3
- point_weight: bfloat16 [384, 768], P('ch'), may hold values from -0.3125 to 0.3125
- point_bias: float32 [768], P('ch'), may hold values from -3 to 3
- cotangent: bfloat16 [32, 1024, 768], P(None, 'seq'), may hold values from -6 to 6
Outputs:
- result: bfloat16 [32, 1024, 768], P(None, 'seq', 'ch')
- input_grad: bfloat16 [32, 2048, 768], P(None, 'seq', 'ch')
- conv_weight_grad: float32 [5, 768, 768], P(None, None, 'ch')
- input_gain_grad: float32 [768], P('ch')
- input_shift_grad: float32 [768], P('ch')
- branch_gain_grad: float32 [768], P('ch')
- branch_shift_grad: float32 [768], P('ch')
- dilated_weight_grad: float32 [3, 768, 384], P(None, None, 'ch')
- mixer_gain_grad: float32 [384], P('ch')
- mixer_shift_grad: float32 [384], P('ch')
- point_weight_grad: float32 [384, 768], P('ch')
- point_bias_grad: float32 [768], P('ch')
Inputs may be any that keep to these rules, and one draw needn't show every extreme that they name: `lengths`: at least one window has all 1024 pooled bins valid.
All inputs are finite; a program needn't handle non-finite values.
Results may differ from a plain program's by a relative error of at most 0.029.
Values may be sent and summed in bfloat16 or wider, within the bound.
A program may use at most 320 MiB of HBM per device.

v0:
```python
from functools import partial
from typing import NamedTuple

import jax
import jax.numpy as jnp
from jax import lax
from jax.experimental import pallas as pl
from jax.experimental.pallas import tpu as pltpu
from jax.sharding import PartitionSpec as P

DIL = 14
EDGE = 16
EPS = 1e-05
GC0 = 0.7978845608028654
GC1 = 0.044715
F32 = jnp.float32
BF16 = jnp.bfloat16
MESH = pl.DeviceIdType.MESH
VMEM_LIMIT = 58 * 1024 * 1024
ANY = pl.BlockSpec(memory_space=pl.ANY)
SMEM = pl.BlockSpec(memory_space=pltpu.SMEM)


ST1, GAIN2, SHIFT2, BIAS, GAIN3, SHIFT3, GAIN1, SHIFT1, ST2, ST3, SU3, BSUM, SU2 = (
    0, 2, 3, 4, 5, 6, 7, 8, 9, 11, 13, 15, 16
)
STATE = 24


class Plan(NamedTuple):
    ns: int
    nz: int
    R: int
    NW: int
    L: int
    C: int
    H: int
    T1: int
    T2: int
    wb: int

    @property
    def g(self):
        return self.nz // self.R

    @property
    def nw(self):
        return self.NW // self.g

    @property
    def Lp(self):
        return self.L // 2

    @property
    def cs(self):
        return self.C // self.nz

    @property
    def Ch(self):
        return self.C // self.R

    @property
    def Hh(self):
        return self.H // self.R

    @property
    def steps(self):
        return self.nw // self.wb

    @property
    def chips(self):
        return self.ns // 2

    @property
    def rb(self):
        return self.cs // self.chips

    def place(self):
        s, z = lax.axis_index("seq"), lax.axis_index("ch")
        return s, z, lax.rem(z, self.g), lax.div(z, self.g)


def gelu(z):
    t = jnp.tanh(z * (GC0 + (GC0 * GC1) * (z * z)))
    return z * (0.5 + 0.5 * t)


def gelu_both(z):
    sq = z * z
    t = jnp.tanh(z * (GC0 + (GC0 * GC1) * sq))
    h = 0.5 + 0.5 * t
    v = z * h
    return v, h + v * (1.0 - t) * (GC0 + (3.0 * GC0 * GC1) * sq)


def gelu_slope(z):
    return gelu_both(z)[1]


def fold(v):
    return jnp.sum(v.reshape(v.shape[0] // 8, 8, v.shape[1]), axis=0)


def fold_lanes(v):
    out = v[:, 0:128]
    for k in range(128, v.shape[1], 128):
        out = out + v[:, k : k + 128]
    return out


def unfold(v):
    return jnp.sum(v, axis=0, keepdims=True)


def rows_of(shape):
    return lax.broadcasted_iota(jnp.int32, shape, 0)


def lanes_of(shape):
    return lax.broadcasted_iota(jnp.int32, shape, 1)


def total_of(lens):
    n = lens[0]
    for k in range(1, lens.shape[0]):
        n = n + lens[k]
    return n.astype(F32)


def norm_of(stats, total):
    mean = stats[0:1] / total
    square = stats[1:2] / total
    return mean, lax.rsqrt(square - mean * mean + EPS)


def flat(ref):
    return ref[...].reshape(1, ref.shape[0])


def column(row, n):
    return jnp.broadcast_to(row, (n, row.shape[1])).T


def mm(a, b):
    return jnp.dot(a, b, preferred_element_type=F32)


def mm_nt(a, b):
    return lax.dot_general(a, b, (((1,), (1,)), ((), ())), preferred_element_type=F32)


def mm_tn(a, b):
    return lax.dot_general(a, b, (((0,), (0,)), ((), ())), preferred_element_type=F32)


def mm_tt(a, b):
    return lax.dot_general(a, b, (((0,), (1,)), ((), ())), preferred_element_type=F32)


def eye_matrix(n, m, first):
    return jnp.where(lanes_of((n, m)) == rows_of((n, m)) + first, 1.0, 0.0).astype(BF16)


def pick_matrix(L):
    r, n = rows_of((L, L)), lanes_of((L, L))
    bin_of = 2 * r - jnp.where(r >= L // 2, L - 1, 0)
    return jnp.where(n == bin_of, 1.0, 0.0).astype(BF16)


def remote(src, dst, send, recv, device):
    return pltpu.make_async_remote_copy(
        src_ref=src,
        dst_ref=dst,
        send_sem=send,
        recv_sem=recv,
        device_id=device,
        device_id_type=MESH,
    )


def wrap(v, n):
    return jnp.where(v >= n, v - n, v)


def greet(devices):
    barrier = pltpu.get_barrier_semaphore()
    for device in devices:
        pl.semaphore_signal(barrier, inc=1, device_id=device, device_id_type=MESH)


def meet(devices):
    pl.semaphore_wait(pltpu.get_barrier_semaphore(), len(devices))


class Peers:
    def __init__(self, me, others):
        self.me, self.others = me, others
        self.count = len(others) + 1

    def start(self, link):
        packet, buf, sems = link
        for device in self.others:
            remote(packet, buf.at[self.me], sems.at[0], sems.at[1], device).start()

    def finish(self, link):
        packet, buf, sems = link
        buf[self.me] = packet[...]
        rest = buf.at[pl.ds(0, self.count - 1)]
        done = remote(rest, rest, sems.at[0], sems.at[1], self.others[0])
        done.wait_recv()
        acc = buf[0]
        for q in range(1, self.count):
            acc = acc + buf[q]
        done.wait_send()
        return acc

    def scratch(self, rows, width):
        return [
            pltpu.VMEM((rows, width), F32),
            pltpu.VMEM((self.count, rows, width), F32),
            pltpu.SemaphoreType.DMA((2,)),
        ]


def group_peers(plan):
    s, z, i, h = plan.place()
    g = plan.g
    others = [
        (wrap(s + a, plan.ns), h * g + wrap(i + b, g))
        for a in range(plan.ns)
        for b in range(g)
        if a or b
    ]
    return Peers(s * g + i, others)


def plane_peers(plan):
    s, z, i, h = plan.place()
    return Peers(s, [(wrap(s + a, plan.ns), z) for a in range(1, plan.ns)])


def line_peers(plan):
    s, z, i, h = plan.place()
    return Peers(z, [(s, wrap(z + a, plan.nz)) for a in range(1, plan.nz)])


class Halo:
    def __init__(self, plan, edge, land, sems):
        self.edge, self.land, self.sems = edge, land, sems
        s, z, _, _ = plan.place()
        self.to = ((wrap(s + plan.ns - 1, plan.ns), z), (wrap(s + 1, plan.ns), z))

    def copy(self, side, rows):
        return remote(
            self.edge.at[side, rows],
            self.land.at[1 - side, rows],
            self.sems.at[0, side],
            self.sems.at[1, side],
            self.to[side],
        )

    def start(self, first, count):
        for side in range(2):
            self.copy(side, pl.ds(first, count)).start()

    def finish(self):
        for side in range(2):
            done = self.copy(side, pl.ds(0, self.land.shape[1]))
            done.wait_recv()
            done.wait_send()


HALO_SEMS = pltpu.SemaphoreType.DMA((2, 2))


class Gather:
    def __init__(self, plan, part, full, sems):
        self.plan, self.part, self.full, self.sems = plan, part, full, sems
        self.s, self.z, self.i, self.h = plan.place()
        self.c, self.m = lax.rem(self.s, 2), lax.div(self.s, 2)
        self.chips = plan.chips
        self.every = self.chips // 4
        self.tap = lax.div(self.m, self.every)
        self.owner = lax.rem(self.m, self.every) == 0
        self.mine = full.at[self.c, self.tap]

    def others(self):
        g, nz = self.plan.g, self.plan.nz
        return [(self.s, wrap(self.h * g + g + r, nz)) for r in range(nz - g)]

    def far(self, off):
        return (2 * wrap(self.m + off, self.chips) + self.c, self.z)

    def line(self, off):
        nz = self.plan.nz
        device = (self.s, wrap(self.z + off, nz))
        dst = self.mine.at[nz - off]
        return remote(self.part, dst, self.sems.at[0, 1], self.sems.at[1, 1], device)

    def far_rows(self, taps):
        return self.full.at[self.c, taps, pl.ds(1, self.plan.nz - 1)]

    def chip(self, off):
        rows = self.far_rows(self.tap)
        return remote(rows, rows, self.sems.at[0, 2], self.sems.at[1, 2], self.far(off))

    def pair(self):
        half = self.far_rows(pl.ds(0, 4))
        device = (2 * self.m + 1 - self.c, self.z)
        return remote(half, half, self.sems.at[0, 3], self.sems.at[1, 3], device)

    def line_start(self):
        @pl.when(self.owner)
        def _():
            for off in range(1, self.plan.nz):
                self.line(off).start()

    def line_finish(self):
        @pl.when(self.owner)
        def _():
            rest = self.far_rows(self.tap)
            device = (self.s, wrap(self.z + 1, self.plan.nz))
            done = remote(rest, rest, self.sems.at[0, 1], self.sems.at[1, 1], device)
            done.wait_recv()
            done.wait_send()

    def chips_start(self):
        @pl.when(self.owner)
        def _():
            for off in range(1, self.chips):
                self.chip(off).start()

    def pair_start(self):
        def taken(count):
            rest = self.far_rows(pl.ds(0, count))
            return remote(rest, rest, self.sems.at[0, 2], self.sems.at[1, 2], self.far(1))

        @pl.when(self.owner)
        def _():
            taken(3).wait_recv()
            for off in range(1, self.chips):
                self.chip(off).wait_send()

        if self.every > 1:

            @pl.when(jnp.logical_not(self.owner))
            def _():
                taken(4).wait_recv()

        self.pair().start()

    def pair_finish(self):
        done = self.pair()
        done.wait_recv()
        done.wait_send()


def first_step():
    return pl.program_id(0) == 0


def last_step():
    return pl.program_id(0) == pl.num_programs(0) - 1


def head_kernel(plan, nm, lens, x, xtop, xend, ctop, cend, g2, s2, pb, g3, s3,
                w_hbm, gain, shift, taps, pw,
                X5, x2, land, state, beyond_out, full,
                macc, beyond, xedge, sel, edge, acc, w_ref, w_sem, part,
                gather_sems, xhalo_sems, halo_sems, *links):
    t = pl.program_id(0)
    peers, plane, line = group_peers(plan), plane_peers(plan), line_peers(plan)
    xhalo = Halo(plan, xedge, beyond, xhalo_sems)
    halo = Halo(plan, edge, land, halo_sems)
    gather = Gather(plan, part, full, gather_sems)
    w_copy = pltpu.make_async_copy(w_hbm, w_ref, w_sem)
    plane_link, line_link, link = links[:3], links[3:6], links[6:]
    s, z, i, h = plan.place()
    L, Lp, C, nw, nz, wb = plan.L, plan.Lp, plan.C, plan.nw, plan.nz, plan.wb
    share = plan.NW // nz
    c = t - nm
    everyone = peers.others + gather.others()

    @pl.when(first_step())
    def _():
        w_copy.start()
        greet(everyone)
        part[...] = jnp.where(gather.tap == 3, pw[...], taps[0])
        macc[...] = jnp.zeros_like(macc)
        acc[...] = jnp.zeros_like(acc)
        state[...] = jnp.zeros_like(state)
        state[GAIN1 : GAIN1 + 1] = flat(gain)
        state[SHIFT1 : SHIFT1 + 1] = flat(shift)
        n16 = nw * 16
        for side, (xe, ce, places) in enumerate(
            ((xtop, ctop, (0, 1, 0)), (xend, cend, (14, 15, 15)))
        ):
            for k, at in enumerate(places):
                rows, lanes = rows_of((nw, n16)), lanes_of((nw, n16))
                one = jnp.where(lanes == 16 * rows + at, 1.0, 0.0).astype(BF16)
                block = (xe if k < 2 else ce)[...].reshape(n16, C)
                xedge[side, k] = mm(one, block)
        shape = (Lp, L)
        for odd in range(2):
            at = lanes_of(shape) - (2 * rows_of(shape) + odd)
            one = jnp.where((at == 0) | (at == 1), 1.0, 0.0)
            sel[odd * Lp : (odd + 1) * Lp] = one.astype(BF16)

    @pl.when(c < 0)
    def _():
        rows = rows_of((L, C))
        for w in range(min(share, wb)):
            at = lax.rem(z * share, wb) + w
            valid = 2 * lens[z * share + t * wb + w] - s * L
            v = jnp.where(rows < valid, x[at].astype(F32), 0.0)
            macc[0] += fold(v)
            macc[1] += fold(v * v)

    @pl.when(c == -1)
    def _():
        packet, more = plane_link[0], line_link[0]
        packet[0:1] = unfold(macc[0])
        packet[1:2] = unfold(macc[1])
        meet(everyone)
        plane.start(plane_link)
        xhalo.start(0, 3)
        at = 0
        spans = []
        more[2:3] = jnp.zeros((1, C), F32)
        for ref in (g2, s2, pb, g3, s3):
            n = ref.shape[1]
            more[2:3, at : at + n] = ref[...]
            spans.append((at, n))
            at += n
        more[0:2] = plane.finish(plane_link)
        line.start(line_link)
        gather.line_start()
        state[ST1 : ST1 + 2] = line.finish(line_link)[0:2]
        for k in range(nz):
            row = line_link[1][k]
            for r, (at, n) in zip((GAIN2, SHIFT2, BIAS, GAIN3, SHIFT3), spans):
                state[r : r + 1, k * n : (k + 1) * n] = row[2:3, at : at + n]
        xhalo.finish()
        beyond_out[...] = beyond[...]
        w_copy.wait()

    @pl.when(c >= 0)
    def _():
        mean, rho = norm_of(state[ST1 : ST1 + 2], 2.0 * total_of(lens))
        scale = state[GAIN1 : GAIN1 + 1] * rho
        offset = state[SHIFT1 : SHIFT1 + 1] - mean * scale
        rows = rows_of((L, C))
        row1 = rows_of((1, C))
        row16 = rows_of((16, C))
        def activate(w):
            at = c * wb + w
            valid = 2 * lens[i * nw + at] - s * L
            a = gelu(x[w].astype(F32) * scale + offset)
            a = jnp.where(rows < valid, a, 0.0).astype(BF16)
            picked = mm(sel[...], a)
            even, odd = picked[0:Lp], picked[Lp:]
            top, end = w * Lp, (w + 1) * Lp
            before = [pltpu.roll(v, 1, 0) for v in (even, odd)]
            behind = pltpu.roll(even, Lp - 1, 0)
            for k, v in enumerate((*before, even, odd, behind)):
                X5[k, top:end] = v.astype(BF16)

            def beside(side, k, bin_at):
                a = gelu(beyond[side, k, pl.ds(at, 1), :] * scale + offset)
                here = (row1 + bin_at < valid) & (row1 + (s * L + bin_at) >= 0)
                return jnp.where(here, a, 0.0).astype(BF16).astype(F32)

            l0, l1 = beside(0, 0, -2), beside(0, 1, -1)
            r0, r1 = beside(1, 0, L), beside(1, 1, L + 1)
            start = a[0:1].astype(F32)
            for k, row in ((0, l0 + l1), (1, l1 + start)):
                X5[k, top : top + 16] = jnp.where(row16 == 0, row, before[k][0:16]).astype(BF16)
            X5[3, end - 16 : end] = (
                odd[Lp - 16 :] + jnp.where(row16 == 15, r0, 0.0)
            ).astype(BF16)
            X5[4, end - 16 : end] = jnp.where(row16 == 15, r0 + r1, behind[Lp - 16 :]).astype(BF16)

        nc = 256
        rowp = rows_of((Lp, nc))

        def convolve(first, count):
            span = slice(first * Lp, (first + count) * Lp)
            for n in range(C // nc):
                cols = slice(n * nc, (n + 1) * nc)
                taps = [X5[k, span] for k in range(plan.T1)]
                y = 0.5 * mm(jnp.concatenate(taps, axis=1), w_ref[:, cols])
                s0 = jnp.zeros((8, nc), F32)
                s1 = jnp.zeros((8, nc), F32)
                for w in range(first, first + count):
                    at = c * wb + w
                    valid = lens[i * nw + at] - s * Lp
                    v = y[(w - first) * Lp : (w - first + 1) * Lp]
                    x2[w, :, cols] = v
                    edge[0, at, :, cols] = v[:EDGE].astype(BF16)
                    edge[1, at, :, cols] = v[Lp - EDGE :].astype(BF16)
                    v = jnp.where(rowp < valid, v, 0.0)
                    s0 = s0 + fold(v)
                    s1 = s1 + fold(v * v)
                acc[0:1, cols] += unfold(s0)
                acc[1:2, cols] += unfold(s1)

        count = max(1, wb // 2)
        for first in range(0, wb, count):
            for w in range(first, first + count):
                activate(w)
            convolve(first, count)
        halo.start(c * wb, wb)

    @pl.when(c == 0)
    def _():
        gather.line_finish()
        gather.chips_start()

    @pl.when(last_step())
    def _():
        link[0][...] = acc[...]
        peers.start(link)
        gather.pair_start()
        state[ST2 : ST2 + 2] = peers.finish(link)
        halo.finish()
        gather.pair_finish()


def block_kernel(plan, lens, x2, x2_hbm, x2land, cot, w_ref, pw_ref, own_w, own_pw, old, half_state,
                 dz2, grads, pgrad, res, land, state, res_got,
                 ext, wf, wt, pw, Y3, c2, dz3, das, a3s, a3T, dos, Z3, dcT,
                 cedge, cland, cacc, dedge, dland, dacc, bedge, bacc, halo_sems, bulk_sems,
                 x2half, x2_sem, *links):
    t = pl.program_id(0)
    peers = group_peers(plan)
    s, z, i, h = plan.place()
    Lp, C, H, wb, nw, cs, g = plan.Lp, plan.C, plan.H, plan.wb, plan.nw, plan.cs, plan.g
    M = wb * Lp
    steps = plan.steps
    p0, r0, b0, g0 = block_phases(plan)[:4]
    c_link, d_link, b_link = links[:3], links[3:6], links[6:]
    c_halo = Halo(plan, cedge, cland, halo_sems.at[0])
    d_halo = Halo(plan, dedge, dland, halo_sems.at[1])
    b_halo = Halo(plan, bedge, land, halo_sems.at[2])

    def bulk(off, rows):
        to = wrap(i + off, g)
        return remote(
            res.at[to, rows],
            res_got.at[off, rows],
            bulk_sems.at[0, off],
            bulk_sems.at[1, off],
            (s, h * g + to),
        )

    def result_of(block):
        y = mm(a3s[pl.ds(pl.multiple_of(block * M, 128), M)], pw[:, pl.ds(pl.multiple_of(h * plan.Ch, 128), plan.Ch)])
        rowr = rows_of((Lp, y.shape[1]))
        for w in range(wb):
            at = block * wb + w
            valid = lens[i * plan.nw + at] - s * Lp
            r = x2half[at] + y[w * Lp : (w + 1) * Lp] + half_state[BIAS : BIAS + 1]
            r = jnp.where(rowr < valid, r, 0.0).astype(BF16).T
            for k in range(g):
                res[k, at] = r[k * cs : (k + 1) * cs]

    def send_result(block):
        result_of(block)
        for off in range(1, g):
            bulk(off, pl.ds(block * wb, wb)).start()

    half_copy = pltpu.make_async_copy(
        x2_hbm.at[:, :, pl.ds(pl.multiple_of(h * plan.Ch, 128), plan.Ch)], x2half, x2_sem
    )

    @pl.when(first_step())
    def _():
        half_copy.start()
        greet(peers.others)
        state[...] = old[...]
        cacc[...] = jnp.zeros_like(cacc)
        dacc[...] = jnp.zeros_like(dacc)
        bacc[...] = jnp.zeros_like(bacc)
        hs = H // plan.nz

        def rows_at(which, first=0):
            return pl.ds(pl.multiple_of(first + which * hs, 16), hs)

        for r in range(plan.nz):
            at = wrap(z + r, plan.nz)
            for c in range(2):
                cols = slice(c * (C // 2), (c + 1) * (C // 2))
                pw[rows_at(at), cols] = own_pw[:, cols] if r == 0 else pw_ref[c, 0, r]
                for k in range(plan.T2):
                    v = own_w[k, :, cols] if r == 0 else w_ref[c, k, r]
                    wf[rows_at(at), k * C + cols.start : k * C + cols.stop] = v
                    wt[rows_at(at, k * H), cols] = v

    @pl.when(t < p0)
    def _():
        base = pl.multiple_of(t * M, 128)
        mean, rho = norm_of(state[ST2 : ST2 + 2], total_of(lens))
        scale = state[GAIN2 : GAIN2 + 1] * rho
        offset = state[SHIFT2 : SHIFT2 + 1] - mean * scale
        rows = rows_of((Lp, C))
        rowe = rows_of((EDGE, C))

        rowh = rows_of((Lp, H))
        sums0, sums1 = jnp.zeros((8, H), F32), jnp.zeros((8, H), F32)
        nh = min(2, wb)
        for first in range(0, wb, wb // nh):
            span = range(first, first + wb // nh)
            for w in span:
                valid = lens[i * plan.nw + t * wb + w] - s * Lp
                a = jnp.where(rows < valid, gelu(x2[w] * scale + offset), 0.0)
                al = gelu(x2land[0, w].astype(F32) * scale + offset)
                al = jnp.where((rowe - EDGE < valid) & (s > 0), al, 0.0)
                ah = gelu(x2land[1, w].astype(F32) * scale + offset)
                ah = jnp.where(rowe + Lp < valid, ah, 0.0)
                ext[w, 0:EDGE] = al
                ext[w, EDGE : EDGE + Lp] = a
                ext[w, EDGE + Lp :] = ah
                top, end = w * Lp, (w + 1) * Lp
                Y3[pl.ds(base + top, Lp), 0:C] = ext[w, EDGE - DIL : EDGE - DIL + Lp].astype(BF16)
                Y3[pl.ds(base + top, Lp), C : 2 * C] = a.astype(BF16)
                Y3[pl.ds(base + top, Lp), 2 * C : 3 * C] = ext[w, EDGE + DIL : EDGE + DIL + Lp].astype(BF16)
            y = mm_nt(Y3[pl.ds(base + first * Lp, wb // nh * Lp)], wf[...])
            for w in span:
                at = t * wb + w
                valid = lens[i * plan.nw + at] - s * Lp
                v = y[(w - first) * Lp : (w - first + 1) * Lp]
                c2[at] = v
                cedge[0, at] = v[:EDGE].astype(BF16)
                cedge[1, at] = v[Lp - EDGE :].astype(BF16)
                v = jnp.where(rowh < valid, v, 0.0)
                sums0 = sums0 + fold(v)
                sums1 = sums1 + fold(v * v)
        cacc[0:1, 0:H] += unfold(sums0)
        cacc[0:1, H:] += unfold(sums1)

    @pl.when(first_step())
    def _():
        meet(peers.others)

    @pl.when(t < p0)
    def _():
        c_halo.start(t * wb, wb)

    @pl.when(t == p0 - 1)
    def _():
        c_link[0][...] = cacc[...]
        peers.start(c_link)

    here_p = (t >= p0) & (t < p0 + steps)

    @pl.when(here_p)
    def _():
        u = t - p0
        rowc = rows_of((Lp, C))
        block = pl.ds(pl.multiple_of(u * M, 128), M)
        bias = jnp.zeros((8, C), F32)
        parts = []
        for w in range(wb):
            valid = lens[i * plan.nw + u * wb + w] - s * Lp
            d = jnp.where(rowc < valid, cot[w].astype(F32), 0.0)
            bias = bias + fold(d)
            parts.append(d.astype(BF16))
        d = jnp.concatenate(parts, axis=0)
        dos[block] = d
        das[...] = mm_nt(d, pw[...])
        dacc[1:2] += unfold(bias)

    @pl.when(t == p0)
    def _():
        got = peers.finish(c_link)
        state[ST3 : ST3 + 1, 0:H] = got[:, 0:H]
        state[ST3 + 1 : ST3 + 2, 0:H] = got[:, H:]

    @pl.when(here_p)
    def _():
        u = t - p0
        block = pl.ds(pl.multiple_of(u * M, 128), M)
        rowh = rows_of((Lp, H))
        mean, rho = norm_of(state[ST3 : ST3 + 2, 0:H], total_of(lens))
        scale = state[GAIN3 : GAIN3 + 1, 0:H] * rho
        offset = state[SHIFT3 : SHIFT3 + 1, 0:H] - mean * scale
        s0, s1 = jnp.zeros((8, H), F32), jnp.zeros((8, H), F32)
        parts = []
        for w in range(wb):
            at = u * wb + w
            valid = lens[i * plan.nw + at] - s * Lp
            top, end = w * Lp, (w + 1) * Lp
            v = c2[at]
            zv = v * scale + offset
            act, slope = gelu_both(zv)
            parts.append(jnp.where(rowh < valid, act, 0.0).astype(BF16))
            dzw = das[top:end] * slope
            dz3[at] = dzw
            dedge[0, at] = dzw[:EDGE].astype(BF16)
            dedge[1, at] = dzw[Lp - EDGE :].astype(BF16)
            s0 = s0 + fold(dzw)
            s1 = s1 + fold(dzw * zv)
        a3 = jnp.concatenate(parts, axis=0)
        a3s[block] = a3
        a3T[:, block] = a3.T
        dacc[0:1, 0:H] += unfold(s0)
        dacc[0:1, H : 2 * H] += unfold(s1)
        d_halo.start(u * wb, wb)

    @pl.when(t == p0)
    def _():
        half_copy.wait()
        send_result(0)

    @pl.when(t == p0 + steps - 1)
    def _():
        d_link[0][...] = dacc[...]
        peers.start(d_link)

    @pl.when(t == r0)
    def _():
        for block in range(1, steps):
            send_result(block)
        rows = pl.ds(pl.multiple_of(h * plan.Hh, 16), plan.Hh)
        pgrad[...] = mm(a3T[rows], dos[...]).astype(BF16)

    @pl.when(t == b0)
    def _():
        got = peers.finish(d_link)
        shift = state[SHIFT3 : SHIFT3 + 1, 0:H]
        gain = state[GAIN3 : GAIN3 + 1, 0:H]
        state[SU3 : SU3 + 1, 0:H] = got[0:1, 0:H]
        state[SU3 + 1 : SU3 + 2, 0:H] = (got[0:1, H : 2 * H] - shift * got[0:1, 0:H]) / gain
        state[BSUM : BSUM + 1] = got[1:2]
        c_halo.finish()
        d_halo.finish()

    @pl.when((t >= b0) & (t < g0))
    def _():
        u = t - b0
        total = total_of(lens)
        mean3, rho3 = norm_of(state[ST3 : ST3 + 2, 0:H], total)
        gr3 = state[GAIN3 : GAIN3 + 1, 0:H] * rho3
        sg3 = state[SU3 : SU3 + 1, 0:H] / total
        gg3 = state[SU3 + 1 : SU3 + 2, 0:H] / total
        mean2, rho2 = norm_of(state[ST2 : ST2 + 2], total)
        scale2 = state[GAIN2 : GAIN2 + 1] * rho2
        offset2 = state[SHIFT2 : SHIFT2 + 1] - mean2 * scale2
        rowh = rows_of((Lp, H))
        rowe = rows_of((EDGE, H))
        rowc = rows_of((Lp, C))

        by_v = -gr3 * rho3 * gg3
        by_1 = gr3 * (mean3 * rho3 * gg3 - sg3)

        def back(dz, v):
            return gr3 * dz + by_v * v + by_1

        for w in range(wb):
            valid = lens[i * nw + u * wb + w] - s * Lp
            d = jnp.where(rowh < valid, back(dz3[u * wb + w], c2[u * wb + w]), 0.0)
            dl = back(dland[0, u * wb + w].astype(F32), cland[0, u * wb + w].astype(F32))
            dl = jnp.where((rowe - EDGE < valid) & (s > 0), dl, 0.0)
            dh = back(dland[1, u * wb + w].astype(F32), cland[1, u * wb + w].astype(F32))
            dh = jnp.where(rowe + Lp < valid, dh, 0.0)
            ext[w, 0:EDGE, 0:H] = dl
            ext[w, EDGE : EDGE + Lp, 0:H] = d
            ext[w, EDGE + Lp :, 0:H] = dh
            top, end = w * Lp, (w + 1) * Lp
            Z3[top:end, 0:H] = ext[w, EDGE + DIL : EDGE + DIL + Lp, 0:H].astype(BF16)
            Z3[top:end, H : 2 * H] = d.astype(BF16)
            Z3[top:end, 2 * H : 3 * H] = ext[w, EDGE - DIL : EDGE - DIL + Lp, 0:H].astype(BF16)

        y = mm(Z3[...], wt[...])

        M = wb * Lp
        dcT[:, pl.ds(pl.multiple_of(u * M, 128), M)] = Z3[:, H : 2 * H].T
        s0, s1 = jnp.zeros((8, C), F32), jnp.zeros((8, C), F32)
        for w in range(wb):
            at = u * wb + w
            valid = lens[i * nw + at] - s * Lp
            v = x2[w]
            zv = v * scale2 + offset2
            dzw = y[w * Lp : (w + 1) * Lp] * gelu_slope(zv)
            dzw = jnp.where(rowc < valid, dzw, 0.0)
            dz2[w] = dzw
            bedge[0, pl.ds(at, 1)] = dzw[0:1]
            bedge[1, pl.ds(at, 1)] = dzw[Lp - 1 : Lp]
            s0 = s0 + fold(dzw)
            s1 = s1 + fold(dzw * zv)
        bacc[0:1] += unfold(s0)
        bacc[1:2] += unfold(s1)

    @pl.when(t == g0 - 1)
    def _():
        b_link[0][...] = bacc[...]
        peers.start(b_link)
        b_halo.start(0, nw)

    @pl.when(last_step())
    def _():
        rows = pl.ds(pl.multiple_of(h * plan.Hh, 16), plan.Hh)
        for n in range(plan.T2):
            cols = slice(n * C, (n + 1) * C)
            grads[:, cols] = mm(dcT[rows], Y3[:, cols]).astype(BF16)

    @pl.when(last_step())
    def _():
        got = peers.finish(b_link)
        shift, gain = state[SHIFT2 : SHIFT2 + 1], state[GAIN2 : GAIN2 + 1]
        state[SU2 : SU2 + 1] = got[0:1]
        state[SU2 + 1 : SU2 + 2] = (got[1:2] - shift * got[0:1]) / gain
        b_halo.finish()
        for off in range(1, g):
            bulk(off, pl.ds(0, nw)).wait()


def block_phases(plan):
    n = plan.steps
    return n, 2 * n, 2 * n + 1, 3 * n + 1, 3 * n + 2


class Reduction:
    def __init__(self, plan, batches, out, give, mine, got, spread, half, mate, sems):
        self.plan, self.batches, self.out = plan, batches, out
        self.give, self.mine, self.got, self.spread = give, mine, got, spread
        self.half, self.mate = half, mate
        self.sems = sems
        self.s, self.z, self.i, self.h = plan.place()
        self.c = lax.rem(self.s, 2)
        self.m = lax.div(self.s, 2)
        self.chips = plan.chips

    @staticmethod
    def scratch(plan, batches):
        taps, wide = plan.T1 + 2, plan.C // 2
        full = (taps, plan.chips, plan.g, plan.rb, wide)
        part = (taps, plan.g, plan.rb, wide)
        return [
            pltpu.VMEM((taps, 2, plan.chips, plan.rb, wide), BF16),
            *[pltpu.VMEM(full, BF16)] * 4,
            *[pltpu.VMEM(part, BF16)] * 2,
            pltpu.SemaphoreType.DMA((2, len(batches), 5)),
        ]

    def copy(self, b, phase, src, dst, device):
        return remote(src, dst, self.sems.at[0, b, phase], self.sems.at[1, b, phase], device)

    def finish(self, b, phase, ref, device):
        done = self.copy(b, phase, ref, ref, device)
        done.wait_recv()
        done.wait_send()

    def taps(self, b):
        return pl.ds(*self.batches[b])

    def pair(self):
        return (2 * self.m + (1 - self.c), self.z)

    def far(self, off):
        return (2 * wrap(self.m + off, self.chips) + self.c, self.z)

    def member(self, off):
        return (self.s, self.h * self.plan.g + wrap(self.i + off, self.plan.g))

    def put(self, k, rows):
        wide = self.plan.C // 2
        for j in range(self.plan.g):
            for m in range(self.chips):
                v = rows(j, m)
                left, right = v[:, :wide], v[:, wide:]
                self.mine[k, m, j] = jnp.where(self.c == 0, left, right).astype(BF16)
                self.give[k, m, j] = jnp.where(self.c == 0, right, left).astype(BF16)

    def step0(self, b):
        taps = self.taps(b)
        self.copy(b, 0, self.give.at[taps], self.got.at[taps], self.pair()).start()

    def step1(self, b):
        taps = self.taps(b)
        self.finish(b, 0, self.got.at[taps], self.pair())
        first, count = self.batches[b]
        for k in range(first, first + count):
            v = self.mine[k].astype(F32) + self.got[k].astype(F32)
            self.mine[k] = v.astype(BF16)
        for off in range(1, self.chips):
            src = self.mine.at[taps, wrap(self.m + off, self.chips)]
            self.copy(b, 1, src, self.spread.at[taps, self.m], self.far(off)).start()

    def step2(self, b):
        taps = self.taps(b)
        self.finish(b, 1, self.spread.at[taps, pl.ds(0, self.chips - 1)], self.far(1))
        first, count = self.batches[b]
        for k in range(first, first + count):
            self.spread[k, self.m] = self.mine[k, self.m]
            v = self.spread[k, 0].astype(F32)
            for n in range(1, self.chips):
                v = v + self.spread[k, n].astype(F32)
            self.half[k] = v.astype(BF16)
        for off in range(1, self.plan.g):
            src = self.half.at[taps, wrap(self.i + off, self.plan.g)]
            self.copy(b, 2, src, self.mate.at[taps, off], self.member(off)).start()

    def step3(self, b):
        taps = self.taps(b)
        self.finish(b, 2, self.mate.at[taps, pl.ds(1, self.plan.g - 1)], self.member(1))
        first, count = self.batches[b]
        for k in range(first, first + count):
            v = self.half[k, self.i].astype(F32)
            for off in range(1, self.plan.g):
                v = v + self.mate[k, off].astype(F32)
            self.out[k, self.c, self.m] = v.astype(BF16)
        mine = self.out.at[taps, self.c, self.m]
        for off in range(1, self.chips):
            self.copy(b, 3, mine, mine, self.far(off)).start()

    def step4(self, b):
        taps = self.taps(b)
        self.finish(b, 3, self.out.at[taps, self.c, pl.ds(0, self.chips - 1)], self.far(1))
        mine = self.out.at[taps, self.c]
        self.copy(b, 4, mine, mine, self.pair()).start()

    def step5(self, b):
        self.finish(b, 4, self.out.at[self.taps(b), self.c], self.pair())


def tail_turns(plan):
    nD, T1 = plan.steps, plan.T1
    turns = [("x", 0)] + [("d", n) for n in range(1, nD)]
    xs, ws = [("x", n) for n in range(1, nD)], [("w", n) for n in range(T1)]
    for count in (2, 1, T1):
        turns += ws[:count] + xs[:1]
        xs, ws = xs[1:], ws[count:]
    return turns + xs


def tail_batches(plan):
    return [(plan.T1, 2), (0, 2)] + [(k, 1) for k in range(2, plan.T1)]


def tail_kernel(plan, lens, dz2, dzland, x2, x2land, cot, beyond, x, X5_hbm, taps_hbm, grads, pgrad,
                old, half_state,
                gz, gz_got, sums, summed,
                ext, D3, D0T, wcat, pick, eye, cols, y, part, split, acc, X5, X5_sems,
                taps, bulk_sems, *rest):
    t = pl.program_id(0)
    s, z, i, h = plan.place()
    L, Lp, C, wb, g, nw = plan.L, plan.Lp, plan.C, plan.wb, plan.g, plan.nw
    Ch, cs, T1 = plan.Ch, plan.cs, plan.T1
    M = wb * Lp
    nD = plan.steps
    turns = tail_turns(plan)
    last = len(turns) - 1
    peers = group_peers(plan)
    red = Reduction(plan, tail_batches(plan), *rest[:8])
    link = rest[8:]

    def member(off):
        return (s, h * g + wrap(i + off, g))

    def send(first, count):
        rows = pl.ds(first, count)
        for off in range(1, g):
            remote(
                part.at[off - 1, rows],
                gz_got.at[off, rows],
                bulk_sems.at[0, off],
                bulk_sems.at[1, off],
                member(off),
            ).start()

    def X5_copy(k):
        return pltpu.make_async_copy(X5_hbm.at[k], X5.at[k % 2], X5_sems.at[k % 2])

    def when(at):
        return pl.when(t == min(at, last))

    def turn(kind, k):
        return turns.index((kind, k)) if (kind, k) in turns else last

    def turn_of(kind):
        index = jnp.int32(0)
        here = False
        for n, (what, k) in enumerate(turns):
            if what == kind:
                index = jnp.where(t == n, k, index)
                here = (t == n) | here
        return here, index

    taps_copy = pltpu.make_async_copy(
        taps_hbm.at[:, pl.ds(pl.multiple_of(h * Ch, 128), Ch)], taps, X5_sems.at[2]
    )

    @when(0)
    def _():
        taps_copy.start()
        greet(peers.others)
        acc[...] = jnp.zeros_like(acc)
        pick[...] = pick_matrix(L)
        eye[...] = eye_matrix(Ch, Ch, 0)
        mean, rho = norm_of(half_state[ST1 : ST1 + 2], 2.0 * total_of(lens))
        scale = half_state[GAIN1 : GAIN1 + 1] * rho
        offset = half_state[SHIFT1 : SHIFT1 + 1] - mean * scale
        for k, row in enumerate((scale, offset)):
            cols[k] = column(row, L)

    @pl.when(t < nD)
    def _():
        total = total_of(lens)
        mean, rho = norm_of(old[ST2 : ST2 + 2], total)
        gr = old[GAIN2 : GAIN2 + 1] * rho
        sg = old[SU2 : SU2 + 1] / total
        gg = old[SU2 + 1 : SU2 + 2] / total
        rowc = rows_of((Lp, C))
        row1 = rows_of((1, C))

        by_dz = 0.5 * gr
        by_v = -0.5 * gr * rho * gg
        by_1 = 0.5 * gr * (mean * rho * gg - sg)

        def back(dout, dz, v):
            return 0.5 * dout + by_dz * dz + by_v * v + by_1

        def grad_of(w):
            at = t * wb + w
            valid = lens[i * nw + at] - s * Lp
            d = back(cot[w].astype(F32), dz2[w], x2[w])
            d = jnp.where(rowc < valid, d, 0.0)
            one = pl.ds(at, 1)
            dl = back(beyond[0, 2, one, :], dzland[0, one, :], x2land[0, w, EDGE - 1 : EDGE].astype(F32))
            dl = jnp.where((row1 - 1 < valid) & (s > 0), dl, 0.0)
            dh = back(beyond[1, 2, one, :], dzland[1, one, :], x2land[1, w, 0:1].astype(F32))
            dh = jnp.where(row1 + Lp < valid, dh, 0.0)
            ext[w, 7:8] = dl
            ext[w, 8 : 8 + Lp] = d
            ext[w, 8 + Lp : 9 + Lp] = dh
            top, end = w * Lp, (w + 1) * Lp
            D3[t, top:end, 0:C] = ext[w, 9 : 9 + Lp].astype(BF16)
            D3[t, top:end, C : 2 * C] = d.astype(BF16)
            D3[t, top:end, 2 * C : 3 * C] = ext[w, 7 : 7 + Lp].astype(BF16)

        for w in range(wb):
            grad_of(w)
        half = D3[t, :, pl.ds(pl.multiple_of(C + h * Ch, 128), Ch)]
        D0T[:, pl.ds(pl.multiple_of(t * M, 128), M)] = half.T

    @when(0)
    def _():
        taps_copy.wait()
        for first in range(0, Ch, 64):
            rows = slice(first, min(first + 64, Ch))
            for r, parts in enumerate((((0,), (1, 2), (3, 4)), ((0, 1), (2, 3), (4,)))):
                for k, which in enumerate(parts):
                    v = taps[which[0], rows]
                    if len(which) > 1:
                        v = (v.astype(F32) + taps[which[1], rows].astype(F32)).astype(BF16)
                    at = r * Ch
                    wcat[at + rows.start : at + rows.stop, k * C : (k + 1) * C] = v
        meet(peers.others)

    here_x, bx = turn_of("x")

    def gradient(hf, nh):
        lanes = lanes_of((Ch, L))

        def through(w):
            valid = 2 * lens[i * nw + bx * wb + w] - s * L
            top, end = w * Lp, (w + 1) * Lp
            v = mm_nt(eye[...], x[w])
            da = jnp.concatenate([y[0:Ch, top:end], y[Ch:, top:end]], axis=1)
            da = mm(da.astype(BF16), pick[...])
            zv = v * cols[0] + cols[1]
            dzw = da * gelu_slope(zv)
            dzw = jnp.where(lanes < valid, dzw, 0.0)
            acc[0] += fold_lanes(dzw)
            acc[1] += fold_lanes(dzw * zv)
            split[w % 2] = dzw.astype(BF16)
            for off in range(g):
                rows = pl.ds(pl.multiple_of(lax.rem(i + off, g) * cs, 16), cs)
                if off == 0:
                    gz[w] = split[w % 2, rows]
                else:
                    part[off - 1, bx * wb + w] = split[w % 2, rows]

        n = wb // nh
        rows = slice(hf * n * Lp, (hf + 1) * n * Lp)
        y[:, rows] = mm_nt(wcat[...], D3[bx, rows])
        for w in range(hf * n, (hf + 1) * n):
            through(w)

    nh = 2 if wb % 2 == 0 and wb * Lp // 2 % 128 == 0 else 1

    @pl.when(here_x)
    def _():
        gradient(0, nh)
        send(bx * wb, wb // nh)

    first = min(1, last)
    table = (
        (first, 1, red.step1, 0),
        (max(turn("w", 1), first + 1), 1, red.step2, 0),
        (turn("w", 1), 1, red.step0, 1),
        (turn("x", 1), 0, red.step1, 1),
        (turn("w", 2), 1, red.step0, 2),
        (turn("x", 2), 0, red.step1, 2),
        (turn("x", 2), 1, red.step3, 0),
        (turn("x", 2), 1, red.step2, 1),
        (turn("w", 3), 1, red.step0, 3),
        (turn("w", 4), 1, red.step0, 4),
        (turn("w", 4), 1, red.step1, 3),
        (turn("w", 4), 1, red.step2, 2),
        (turn("x", 3), 0, red.step1, 4),
        (turn("x", 3), 0, red.step4, 0),
        (turn("x", 3), 0, red.step3, 1),
        (last, 1, red.step2, 3),
        (last, 1, red.step3, 2),
        (last, 1, red.step2, 4),
    )

    def between(at, end):
        return end == 0 and nh == 2 and turns[at][0] == "x"

    def go_on(entries):
        for at, _, step, batch in entries:

            @when(at)
            def _():
                step(batch)

    go_on([e for e in table if between(*e[:2])])

    if nh == 2:

        @pl.when(here_x)
        def _():
            gradient(1, nh)

    @when(0)
    def _():
        hs = plan.H // plan.nz
        rb = plan.rb
        for u in range(2):

            def rows(j, m, u=u):
                side, r = m * rb // hs, m * rb % hs
                n = 2 * side + u
                rows = slice(j * hs + r, j * hs + r + rb)
                v = grads[rows, n * C : (n + 1) * C] if n < plan.T2 else pgrad[rows]
                return v.astype(F32)

            red.put(T1 + u, rows)
        red.step0(0)

    @when(1)
    def _():
        X5_copy(0).start()
        X5_copy(1).start()

    here_w, k = turn_of("w")

    @pl.when(here_w)
    def _():
        X5_copy(k).wait()
        y[0:Ch, 0:C] = mm(D0T[...], X5[lax.rem(k, 2)])

        @pl.when(k < T1 - 2)
        def _():
            X5_copy(k + 2).start()

        rb = plan.rb
        red.put(k, lambda j, m: y[j * cs + m * rb : j * cs + (m + 1) * rb, 0:C])

    @when(turn("x", nD - 1))
    def _():
        packet = link[0]
        packet[...] = jnp.zeros_like(packet)
        packet[0:1, 0:Ch] = jnp.sum(acc[0].T, axis=0, keepdims=True)
        packet[1:2, 0:Ch] = jnp.sum(acc[1].T, axis=0, keepdims=True)
        peers.start(link)

    go_on([e for e in table if not between(*e[:2])])

    @pl.when(here_x & (bx < nD - 1))
    def _():
        if nh == 2:
            send(bx * wb + wb // nh, wb // nh)

    @when(last)
    def _():
        if nh == 2:
            send(nw - wb // 2, wb // 2)

    @when(last)
    def _():
        red.step3(3)
        red.step4(1)
        red.step4(2)
        red.step3(4)
        red.step4(3)
        got = peers.finish(link)[:, 0:Ch]
        shift, gain = half_state[SHIFT1 : SHIFT1 + 1], half_state[GAIN1 : GAIN1 + 1]
        sums[0:1] = got[0:1]
        sums[1:2] = (got[1:2] - shift * got[0:1]) / gain
        red.step4(4)
        for b in range(5):
            red.step5(b)
        own = pltpu.make_async_copy(red.out, summed, X5_sems.at[0])
        own.start()
        for off in range(1, g):
            done = remote(
                part.at[off - 1],
                gz_got.at[off],
                bulk_sems.at[0, off],
                bulk_sems.at[1, off],
                member(off),
            )
            done.wait_recv()
            done.wait_send()
        own.wait()


def input_grad_kernel(plan, wg, lens, x, gz, gz_got, sums, res, res_got, summed,
                      state, half_state,
                      out, out_result, conv_grad, dil_grad, point_grad,
                      g1, b1, g2, b2, g3, b3, pb, eye, cols, xt):
    t = pl.program_id(0)
    s, z, i, h = plan.place()
    L, Ch, cs = plan.L, plan.Ch, plan.cs
    turn = plan.nw // wg
    mine = pl.ds(pl.multiple_of(i * cs, 16), cs)

    @pl.when(first_step())
    def _():
        n = 2.0 * total_of(lens)
        mean, rho = norm_of(half_state[ST1 : ST1 + 2], n)
        gr = half_state[GAIN1 : GAIN1 + 1] * rho
        gg = sums[1:2] / n * rho
        for k, row in enumerate((gr, -gr * gg, gr * (mean * gg - sums[0:1] / n))):
            xt[...] = column(row, L)
            cols[k] = xt[mine]
        eye[...] = eye_matrix(cs, Ch, i * cs)

        def mine_of(src, at, which, count, *dsts):
            n = dsts[0].shape[1]
            for k in range(count):

                @pl.when(which == k)
                def _():
                    for dst, r in zip(dsts, at):
                        dst[...] = src[r : r + 1, k * n : (k + 1) * n]

        mine_of(sums, (1, 0), i, plan.g, g1, b1)
        mine_of(state, (SU2 + 1, SU2), z, plan.nz, g2, b2)
        mine_of(state, (SU3 + 1, SU3), z, plan.nz, g3, b3)
        mine_of(state, (BSUM,), z, plan.nz, pb)

    own = lax.div(t, turn) == i
    for w in range(wg):
        out_result[w] = jnp.where(own, res[0, w], res_got[0, w])

    C, T1, hs, rb, wide = plan.C, plan.T1, plan.H // plan.nz, plan.rb, plan.C // 2
    count = plan.NW // wg
    turns = min(count, plan.chips)
    per, every = plan.chips // turns, count // turns

    def spread(chunk):
        for n in range(per):
            m = chunk * per + n
            side, r = m * rb // hs, m * rb % hs
            for c in range(2):
                at = slice(c * wide, (c + 1) * wide)
                for k in range(T1):
                    conv_grad[k, n * rb : (n + 1) * rb, at] = summed[k, c, n].astype(F32)
                for u in range(2):
                    v = summed[T1 + u, c, n].astype(F32)
                    if 2 * side + u < plan.T2:
                        dil_grad[2 * side + u, r : r + rb, at] = v
                    else:
                        point_grad[r : r + rb, at] = v

    for chunk in range(turns):
        pl.when(t == chunk * every)(partial(spread, chunk))

    lanes = lanes_of((cs, L))
    for w in range(wg):
        valid = 2 * lens[t * wg + w] - s * L
        v = mm_nt(eye[...], x[w])
        dz = jnp.where(own, gz[w], gz_got[0, w]).astype(F32)
        r = cols[0] * dz + v * cols[1] + cols[2]
        out[w] = jnp.where(lanes < valid, r, 0.0).astype(BF16)


def call(kernel, plan, name, steps, ins, outs, scratch, flops, nbytes, cid=None):
    extra = {} if cid is None else dict(collective_id=cid, has_side_effects=True)
    return pl.pallas_call(
        partial(kernel, plan),
        grid=(steps,),
        in_specs=[SMEM] + [spec for spec, _ in ins],
        out_specs=[spec for spec, _, _ in outs],
        out_shape=[jax.ShapeDtypeStruct(shape, dtype) for _, shape, dtype in outs],
        scratch_shapes=scratch,
        compiler_params=pltpu.CompilerParams(vmem_limit_bytes=VMEM_LIMIT, **extra),
        cost_estimate=pl.CostEstimate(
            flops=int(flops), bytes_accessed=int(nbytes), transcendentals=0
        ),
        name=name,
    )


def per_device(
    inputs,
    lengths,
    input_gain,
    input_shift,
    conv_weight,
    branch_gain,
    branch_shift,
    dilated_tap_weight,
    mixer_gain,
    mixer_shift,
    point_weight,
    point_bias,
    cotangent,
):
    NW, L, C = inputs.shape
    Lp = L // 2
    nz = lax.axis_size("ch")
    R = 2
    plan = Plan(
        ns=lax.axis_size("seq"),
        nz=nz,
        R=R,
        NW=NW,
        L=L,
        C=C,
        H=mixer_gain.shape[0] * nz,
        T1=conv_weight.shape[0],
        T2=dilated_tap_weight.shape[0],
        wb=min(NW * R // nz, max(1, 512 // Lp)),
    )
    g, nw, cs, Ch, H, Hh, wb = plan.g, plan.nw, plan.cs, plan.Ch, plan.H, plan.Hh, plan.wb
    T1, T2, steps = plan.T1, plan.T2, plan.steps
    M = wb * Lp
    hs = H // nz
    lens = lengths.astype(jnp.int32)

    def row(a):
        return a.reshape(1, a.shape[0])

    def grp():
        return lax.rem(lax.axis_index("ch"), g)

    def half():
        return lax.div(lax.axis_index("ch"), g)

    def core():
        return lax.rem(lax.axis_index("seq"), 2)

    def chip4():
        return lax.div(lax.axis_index("seq"), plan.ns // 4)

    def whole(*shape):
        return pl.BlockSpec(shape, lambda t: (0,) * len(shape), pipeline_mode=pl.Buffered(1))

    def const(*shape):
        return pl.BlockSpec(shape, lambda t: (0,) * len(shape))

    def win(*shape):
        return pl.BlockSpec(shape, lambda t: (t,) + (0,) * (len(shape) - 1))

    def arg_win(n, width):
        return pl.BlockSpec((wb, n, width), lambda t: (grp() * steps + t, 0, 0))

    def ins(*pairs):
        return [p for p in pairs]

    share = NW // nz
    nm = max(1, share // wb)

    def edge_spec(n):
        return pl.BlockSpec(
            (nw, 16, C), lambda t: (grp(), n, 0), pipeline_mode=pl.Buffered(1)
        )

    def head_block(t):
        own = lax.div(lax.axis_index("ch") * share, wb) + t
        return jnp.where(t < nm, own, grp() * steps + t - nm), 0, 0

    def after(*shape):
        return pl.BlockSpec(
            shape, lambda t: (jnp.maximum(t - nm, 0),) + (0,) * (len(shape) - 1)
        )

    pairs = ins(
        (pl.BlockSpec((wb, L, C), head_block), inputs),
        (edge_spec(0), inputs),
        (edge_spec(L // 16 - 1), inputs),
        (edge_spec(0), cotangent),
        (edge_spec(Lp // 16 - 1), cotangent),
        (whole(1, cs), row(branch_gain)),
        (whole(1, cs), row(branch_shift)),
        (whole(1, cs), row(point_bias)),
        (whole(1, H // nz), row(mixer_gain)),
        (whole(1, H // nz), row(mixer_shift)),
        (ANY, conv_weight.reshape(T1 * C, C)),
        (whole(C), input_gain),
        (whole(C), input_shift),
        (
            pl.BlockSpec(
                (1, hs, C // 2),
                lambda t: (jnp.minimum(chip4(), T2 - 1), 0, core()),
                pipeline_mode=pl.Buffered(1),
            ),
            jnp.swapaxes(dilated_tap_weight, 1, 2),
        ),
        (
            pl.BlockSpec(
                (hs, C // 2), lambda t: (0, core()), pipeline_mode=pl.Buffered(1)
            ),
            point_weight,
        ),
    )
    plane, line, group = plane_peers(plan), line_peers(plan), group_peers(plan)
    state_shape = (STATE, C)
    edges2, edges3 = (2, nw, EDGE, C), (2, nw, EDGE, H)
    X5, x2, land2, state, beyond, full = call(
        lambda plan, *refs: head_kernel(plan, nm, *refs),
        plan,
        "head",
        nm + steps,
        pairs,
        [
            (
                pl.BlockSpec((T1, M, C), lambda t: (0, jnp.maximum(t - nm, 0), 0)),
                (T1, nw * Lp, C),
                BF16,
            ),
            (after(wb, Lp, C), (nw, Lp, C), F32),
            (ANY, edges2, BF16),
            (const(*state_shape), state_shape, F32),
            (const(2, 3, nw, C), (2, 3, nw, C), F32),
            (ANY, (2, T2 + 1, nz, hs, C // 2), BF16),
        ],
        [
            pltpu.VMEM((2, 8, C), F32),
            pltpu.VMEM((2, 3, nw, C), F32),
            pltpu.VMEM((2, 3, nw, C), F32),
            pltpu.VMEM((L, L), BF16),
            pltpu.VMEM(edges2, BF16),
            pltpu.VMEM((2, C), F32),
            pltpu.VMEM((T1 * C, C), BF16),
            pltpu.SemaphoreType.DMA,
            pltpu.VMEM((hs, C // 2), BF16),
            pltpu.SemaphoreType.DMA((2, 4)),
            HALO_SEMS,
            HALO_SEMS,
        ]
        + plane.scratch(2, C)
        + line.scratch(3, C)
        + group.scratch(2, C),
        2 * nw * Lp * T1 * C * C,
        nw * Lp * C * 20,
        cid=1,
    )(lens, *[a for _, a in pairs])

    taps_spec = whole(2, T2, nz, hs, C // 2)
    pw_spec = pl.BlockSpec(
        (2, 1, nz, hs, C // 2), lambda t: (0, T2, 0, 0, 0), pipeline_mode=pl.Buffered(1)
    )

    def early(*shape):
        return pl.BlockSpec(
            shape, lambda t: (jnp.minimum(t, steps - 1),) + (0,) * (len(shape) - 1)
        )

    def early_land(width):
        return pl.BlockSpec(
            (2, wb, EDGE, width), lambda t: (0, jnp.minimum(t, steps - 1), 0, 0)
        )

    def half_of(n):
        return pl.BlockSpec((n, Ch), lambda t: (0, half()), pipeline_mode=pl.Buffered(1))

    cot_spec = pl.BlockSpec(
        (wb, Lp, C), lambda t: (grp() * steps + jnp.minimum(t, steps - 1), 0, 0)
    )

    p0, r0, b0, g0, block_steps = block_phases(plan)

    def at_phase(first):
        return lambda t: jnp.clip(t - first, 0, steps - 1)

    in_p, in_b = at_phase(p0), at_phase(b0)
    pairs = ins(
        (
            pl.BlockSpec(
                (wb, Lp, C),
                lambda t: (jnp.where(t < p0 + steps, jnp.minimum(t, steps - 1), in_b(t)), 0, 0),
            ),
            x2,
        ),
        (ANY, x2),
        (early_land(C), land2),
        (pl.BlockSpec((wb, Lp, C), lambda t: (grp() * steps + in_p(t), 0, 0)), cotangent),
        (taps_spec, full),
        (pw_spec, full),
        (whole(T2, hs, C), jnp.swapaxes(dilated_tap_weight, 1, 2)),
        (whole(hs, C), point_weight),
        (whole(*state_shape), state),
        (half_of(STATE), state),
    )
    dz2, grads, pgrad, res, dland2, state, res_got = call(
        block_kernel,
        plan,
        "block",
        block_steps,
        pairs,
        [
            (pl.BlockSpec((wb, Lp, C), lambda t: (in_b(t), 0, 0)), (nw, Lp, C), F32),
            (const(Hh, T2 * C), (Hh, T2 * C), BF16),
            (const(Hh, C), (Hh, C), BF16),
            (const(g, nw, cs, Lp), (g, nw, cs, Lp), BF16),
            (ANY, (2, nw, C), F32),
            (const(*state_shape), state_shape, F32),
            (ANY, (g, nw, cs, Lp), BF16),
        ],
        [
            pltpu.VMEM((wb, Lp + 2 * EDGE, C), F32),
            pltpu.VMEM((H, T2 * C), BF16),
            pltpu.VMEM((T2 * H, C), BF16),
            pltpu.VMEM((H, C), BF16),
            pltpu.VMEM((nw * Lp, T2 * C), BF16),
            pltpu.VMEM((nw, Lp, H), F32),
            pltpu.VMEM((nw, Lp, H), F32),
            pltpu.VMEM((M, H), F32),
            pltpu.VMEM((nw * Lp, H), BF16),
            pltpu.VMEM((H, nw * Lp), BF16),
            pltpu.VMEM((nw * Lp, C), BF16),
            pltpu.VMEM((M, T2 * H), BF16),
            pltpu.VMEM((H, nw * Lp), BF16),
            pltpu.VMEM(edges3, BF16),
            pltpu.VMEM(edges3, BF16),
            pltpu.VMEM((1, 2 * H), F32),
            pltpu.VMEM(edges3, BF16),
            pltpu.VMEM(edges3, BF16),
            pltpu.VMEM((2, C), F32),
            pltpu.VMEM((2, nw, C), F32),
            pltpu.VMEM((2, C), F32),
            pltpu.SemaphoreType.DMA((3, 2, 2)),
            pltpu.SemaphoreType.DMA((2, g)),
            pltpu.VMEM((nw, Lp, Ch), F32),
            pltpu.SemaphoreType.DMA,
        ]
        + group.scratch(1, 2 * H)
        + group.scratch(2, C)
        + group.scratch(2, C),
        nw * Lp * C * H * (6 * T2 + 6),
        nw * Lp * C * 30,
        cid=3,
    )(lens, *[a for _, a in pairs])

    chips, rb = plan.chips, plan.rb
    turns_t = tail_turns(plan)

    def x_block(t):
        block = jnp.int32(0)
        for n, (what, k) in enumerate(turns_t):
            if what == "x":
                block = jnp.where(t >= n, k, block)
        return block

    sshape = (T1 + 2, 2, chips, rb, C // 2)
    pairs = ins(
        (early(wb, Lp, C), dz2),
        (whole(2, nw, C), dland2),
        (early(wb, Lp, C), x2),
        (early_land(C), land2),
        (cot_spec, cotangent),
        (whole(2, 3, nw, C), beyond),
        (
            pl.BlockSpec(
                (wb, L, Ch), lambda t: (grp() * steps + x_block(t), 0, half())
            ),
            inputs,
        ),
        (ANY, X5),
        (ANY, conv_weight),
        (whole(Hh, T2 * C), grads),
        (whole(Hh, C), pgrad),
        (whole(*state_shape), state),
        (half_of(STATE), state),
    )
    gz, gz_got, sums1, summed = call(
        tail_kernel,
        plan,
        "tail",
        len(turns_t),
        pairs,
        [
            (pl.BlockSpec((wb, cs, L), lambda t: (x_block(t), 0, 0)), (nw, cs, L), BF16),
            (ANY, (g, nw, cs, L), BF16),
            (const(2, Ch), (2, Ch), F32),
            (ANY, sshape, BF16),
        ],
        [
            pltpu.VMEM((wb, Lp + 16, C), F32),
            pltpu.VMEM((steps, M, 3 * C), BF16),
            pltpu.VMEM((Ch, nw * Lp), BF16),
            pltpu.VMEM((2 * Ch, 3 * C), BF16),
            pltpu.VMEM((L, L), BF16),
            pltpu.VMEM((Ch, Ch), BF16),
            pltpu.VMEM((2, Ch, L), F32),
            pltpu.VMEM((2 * Ch, max(M, C)), F32),
            pltpu.VMEM((g - 1, nw, cs, L), BF16),
            pltpu.VMEM((2, Ch, L), BF16),
            pltpu.VMEM((2, Ch, min(L, 128)), F32),
            pltpu.VMEM((2, nw * Lp, C), BF16),
            pltpu.SemaphoreType.DMA((3,)),
            pltpu.VMEM((T1, Ch, C), BF16),
            pltpu.SemaphoreType.DMA((2, g)),
        ]
        + Reduction.scratch(plan, tail_batches(plan))
        + group.scratch(2, C),
        2 * nw * Lp * (6 + T1) * C * Ch,
        nw * Lp * C * 40,
        cid=6,
    )(lens, *[a for _, a in pairs])

    wg = min(2 * wb, nw)
    count = NW // wg
    turn = nw // wg
    turns = min(count, chips)

    def own_block(t):
        return jnp.where(lax.div(t, turn) == grp(), lax.rem(t, turn), 0)

    def got_slot(t):
        off = lax.rem(grp() - lax.div(t, turn) + g, g)
        return jnp.maximum(off, 1), jnp.where(off > 0, lax.rem(t, turn), 0)

    pairs = ins(
        (pl.BlockSpec((wg, L, Ch), lambda t: (t, 0, half())), inputs),
        (pl.BlockSpec((wg, cs, L), lambda t: (own_block(t), 0, 0)), gz),
        (pl.BlockSpec((1, wg, cs, L), lambda t: got_slot(t) + (0, 0)), gz_got),
        (whole(2, Ch), sums1),
        (pl.BlockSpec((1, wg, cs, Lp), lambda t: (grp(), own_block(t), 0, 0)), res),
        (pl.BlockSpec((1, wg, cs, Lp), lambda t: got_slot(t) + (0, 0)), res_got),
        (
            pl.BlockSpec(
                (T1 + 2, 2, chips // turns, rb, C // 2),
                lambda t: (0, 0, t * turns // count, 0, 0),
            ),
            summed,
        ),
        (whole(*state_shape), state),
        (half_of(STATE), state),
    )
    outs = call(
        lambda plan, *refs: input_grad_kernel(plan, wg, *refs),
        plan,
        "input_grad",
        count,
        pairs,
        [
            (win(wg, cs, L), (NW, cs, L), BF16),
            (win(wg, cs, Lp), (NW, cs, Lp), BF16),
            (
                pl.BlockSpec((T1, cs // turns, C), lambda t: (0, t * turns // count, 0)),
                (T1, cs, C),
                F32,
            ),
            (const(T2, hs, C), (T2, hs, C), F32),
            (const(hs, C), (hs, C), F32),
        ]
        + [(const(1, n), (1, n), F32) for n in (cs, cs, cs, cs, hs, hs, cs)],
        [
            pltpu.VMEM((cs, Ch), BF16),
            pltpu.VMEM((3, cs, L), F32),
            pltpu.VMEM((Ch, L), F32),
        ],
        2 * NW * L * Ch * cs,
        NW * L * cs * 8,
    )(lens, *[a for _, a in pairs])
    grad, result, conv_grad, dil_grad, point_grad = outs[:5]
    g1, b1, g2, b2, g3, b3, pb = [a[0] for a in outs[5:]]
    return (
        jnp.swapaxes(result, 1, 2),
        jnp.swapaxes(grad, 1, 2),
        jnp.swapaxes(conv_grad, 1, 2),
        g1,
        b1,
        g2,
        b2,
        jnp.swapaxes(dil_grad, 1, 2),
        g3,
        b3,
        point_grad,
        pb,
    )


def solution(mesh):
    in_specs = (
        P(None, "seq", None),
        P(),
        P(),
        P(),
        P(),
        P("ch"),
        P("ch"),
        P(None, None, "ch"),
        P("ch"),
        P("ch"),
        P("ch", None),
        P("ch"),
        P(None, "seq", None),
    )
    out_specs = (
        P(None, "seq", "ch"),
        P(None, "seq", "ch"),
        P(None, None, "ch"),
        P("ch"),
        P("ch"),
        P("ch"),
        P("ch"),
        P(None, None, "ch"),
        P("ch"),
        P("ch"),
        P("ch", None),
        P("ch"),
    )
    return jax.shard_map(
        per_device, mesh=mesh, in_specs=in_specs, out_specs=out_specs, check_vma=False
    )
```

profile of v0, /device:TPU:0, one launch (start us, length us, event | category | flops | bytes accessed | tf_op | source)
XLA Modules:
  0.0 163.5 jit_solution(10604517707226146806)
XLA Ops:
  0.6 46.8 %head.1 = (bf16[5,2048,768]{2,1,0:T(8,128)(2,1)}, f32[16,128,768]{2,1,0:T(8,128)}, bf16[2,16,16,768]{3,2,1,0:T(8,128)(2,1)}, f32[24,768]{1,0:T(8,128)}, f32[2,3,...) custom-call(s32[32]{0:T(128)} %refs_0_.3, bf16[32,256,768]{2,1,0:T(8,128)(2,1)} %refs_1_.3, ...), custom_call_target="tpu_custom_call" | custom-call | flops 12079595520 | bytes 31457280 | tf_op jit(solution)/shard_map/head/pallas_call | solution.py:1426
  47.4 44.6 %block.1 = (f32[16,128,768]{2,1,0:T(8,128)}, bf16[192,2304]{1,0:T(8,128)(2,1)}, bf16[192,768]{1,0:T(8,128)(2,1)}, bf16[2,16,192,128]{3,2,1,0:T(8,128)(2,1)}, f32...) custom-call(s32[32]{0:T(128)} %refs_0_.3, f32[16,128,768]{2,1,0:T(8,128)} %get-tuple-element.41.x2.x2_hbm, ...), custom_call_target="tpu_custom_call" | custom-call | flops 14495514624 | bytes 47185920 | tf_op jit(solution)/shard_map/block/pallas_call | solution.py:1512
  92.0 60.7 %tail.1 = (bf16[16,192,256]{2,1,0:T(8,128)(2,1)}, bf16[2,16,192,256]{3,2,1,0:T(8,128)(2,1)}, f32[2,384]{1,0:T(2,128)}, bf16[7,2,4,48,384]{4,3,2,1,0:T(8,128)(2,1)}) custom-call(s32[32]{0:T(128)} %refs_0_.3, f32[16,128,768]{2,1,0:T(8,128)} %get-tuple-element.45.dz2, f32[2,16,768]{2,1,0:T(8,128)} %get-tuple-element.46.dzland, ...), custom_call_target="tpu_custom_call" | custom-call | flops 13287555072 | bytes 62914560 | tf_op jit(solution)/shard_map/tail/pallas_call | solution.py:1593
  152.7 10.6 %input_grad.1 = (bf16[32,192,256]{2,1,0:T(8,128)(2,1)}, bf16[32,192,128]{2,1,0:T(8,128)(2,1)}, f32[5,192,768]{2,1,0:T(8,128)}, f32[3,96,768]{2,1,0:T(8,128)}, f3...) custom-call(s32[32]{0:T(128)} %refs_0_.3, ...), custom_call_target="tpu_custom_call" | custom-call | flops 1207959552 | bytes 12582912 | tf_op jit(solution)/shard_map/input_grad/pallas_call | solution.py:1658
where the time goes:
time: 164 us; the launch traced here: 163 us
  Pallas kernels  163 us (99%)
    pallas_call x1, Pallas kernels, per_device(): call(tail_kernel, plan, 'tail', len(turns_t), pairs, [(pl.BlockSpec((wb,...  60.7 us
    pallas_call x1, Pallas kernels, per_device(): call(lambda plan, *refs: head_kernel(plan, nm, *refs), plan, 'head', nm +...  46.8 us
    pallas_call x1, Pallas kernels, per_device(): call(block_kernel, plan, 'block', block_steps, pairs, [(pl.BlockSpec((wb,...  44.6 us
    pallas_call x1, Pallas kernels, per_device(): call(lambda plan, *refs: input_grad_kernel(plan, wg, *refs), plan, 'input...  10.6 us

commit v1 on v0

--- a/solution.py
+++ b/solution.py
@@ -941,7 +941,7 @@
 def tail_kernel(plan, lens, dz2, dzland, x2, x2land, cot, beyond, x, X5_hbm, taps_hbm, grads, pgrad,
                 old, half_state,
                 gz, gz_got, sums, summed,
-                ext, D3, D0T, wcat, pick, eye, cols, y, part, split, acc, X5, X5_sems,
+                D3, D0T, wcat, pick, cols, y, part, split, acc, X5, X5_sems,
                 taps, bulk_sems, *rest):
     t = pl.program_id(0)
     s, z, i, h = plan.place()
@@ -997,7 +997,6 @@
         greet(peers.others)
         acc[...] = jnp.zeros_like(acc)
         pick[...] = pick_matrix(L)
-        eye[...] = eye_matrix(Ch, Ch, 0)
         mean, rho = norm_of(half_state[ST1 : ST1 + 2], 2.0 * total_of(lens))
         scale = half_state[GAIN1 : GAIN1 + 1] * rho
         offset = half_state[SHIFT1 : SHIFT1 + 1] - mean * scale
@@ -1013,6 +1012,7 @@
         gg = old[SU2 + 1 : SU2 + 2] / total
         rowc = rows_of((Lp, C))
         row1 = rows_of((1, C))
+        row16 = rows_of((16, C))
 
         by_dz = 0.5 * gr
         by_v = -0.5 * gr * rho * gg
@@ -1031,13 +1031,12 @@
             dl = jnp.where((row1 - 1 < valid) & (s > 0), dl, 0.0)
             dh = back(beyond[1, 2, one, :], dzland[1, one, :], x2land[1, w, 0:1].astype(F32))
             dh = jnp.where(row1 + Lp < valid, dh, 0.0)
-            ext[w, 7:8] = dl
-            ext[w, 8 : 8 + Lp] = d
-            ext[w, 8 + Lp : 9 + Lp] = dh
             top, end = w * Lp, (w + 1) * Lp
-            D3[t, top:end, 0:C] = ext[w, 9 : 9 + Lp].astype(BF16)
-            D3[t, top:end, C : 2 * C] = d.astype(BF16)
-            D3[t, top:end, 2 * C : 3 * C] = ext[w, 7 : 7 + Lp].astype(BF16)
+            after, before = pltpu.roll(d, Lp - 1, 0), pltpu.roll(d, 1, 0)
+            for n, v in enumerate((after, d, before)):
+                D3[t, top:end, n * C : (n + 1) * C] = v.astype(BF16)
+            D3[t, end - 16 : end, 0:C] = jnp.where(row16 == 15, dh, after[Lp - 16 :]).astype(BF16)
+            D3[t, top : top + 16, 2 * C :] = jnp.where(row16 == 0, dl, before[0:16]).astype(BF16)
 
         for w in range(wb):
             grad_of(w)
@@ -1066,7 +1065,7 @@
         def through(w):
             valid = 2 * lens[i * nw + bx * wb + w] - s * L
             top, end = w * Lp, (w + 1) * Lp
-            v = mm_nt(eye[...], x[w])
+            v = x[w].T.astype(F32)
             da = jnp.concatenate([y[0:Ch, top:end], y[Ch:, top:end]], axis=1)
             da = mm(da.astype(BF16), pick[...])
             zv = v * cols[0] + cols[1]
@@ -1603,12 +1602,10 @@
             (ANY, sshape, BF16),
         ],
         [
-            pltpu.VMEM((wb, Lp + 16, C), F32),
             pltpu.VMEM((steps, M, 3 * C), BF16),
             pltpu.VMEM((Ch, nw * Lp), BF16),
             pltpu.VMEM((2 * Ch, 3 * C), BF16),
             pltpu.VMEM((L, L), BF16),
-            pltpu.VMEM((Ch, Ch), BF16),
             pltpu.VMEM((2, Ch, L), F32),
             pltpu.VMEM((2 * Ch, max(M, C)), F32),
             pltpu.VMEM((g - 1, nw, cs, L), BF16),

time: 164 us -> 163 us (level)
  no operation moved by 1% of the time
where the time goes in v1:
time: 163 us
  Pallas kernels  162 us (99%)
    pallas_call x1, Pallas kernels, per_device(): call(tail_kernel, plan, 'tail', len(turns_t), pairs, [(pl.BlockSpec((wb,...  60 us
    pallas_call x1, Pallas kernels, per_device(): call(lambda plan, *refs: head_kernel(plan, nm, *refs), plan, 'head', nm +...  46.8 us
    pallas_call x1, Pallas kernels, per_device(): call(block_kernel, plan, 'block', block_steps, pairs, [(pl.BlockSpec((wb,...  44.6 us
    pallas_call x1, Pallas kernels, per_device(): call(lambda plan, *refs: input_grad_kernel(plan, wg, *refs), plan, 'input...  10.6 us

profile of v1, /device:TPU:0, one launch (start us, length us, event | category | flops | bytes accessed | tf_op | source)
XLA Modules:
  0.0 162.8 jit_solution(6961492479128267063)
XLA Ops:
  0.6 46.8 %head.1 = (bf16[5,2048,768]{2,1,0:T(8,128)(2,1)}, f32[16,128,768]{2,1,0:T(8,128)}, bf16[2,16,16,768]{3,2,1,0:T(8,128)(2,1)}, f32[24,768]{1,0:T(8,128)}, f32[2,3,...) custom-call(s32[32]{0:T(128)} %refs_0_.3, bf16[32,256,768]{2,1,0:T(8,128)(2,1)} %refs_1_.3, ...), custom_call_target="tpu_custom_call" | custom-call | flops 12079595520 | bytes 31457280 | tf_op jit(solution)/shard_map/head/pallas_call | solution.py:1425
  47.4 44.6 %block.1 = (f32[16,128,768]{2,1,0:T(8,128)}, bf16[192,2304]{1,0:T(8,128)(2,1)}, bf16[192,768]{1,0:T(8,128)(2,1)}, bf16[2,16,192,128]{3,2,1,0:T(8,128)(2,1)}, f32...) custom-call(s32[32]{0:T(128)} %refs_0_.3, f32[16,128,768]{2,1,0:T(8,128)} %get-tuple-element.41.x2.x2_hbm, ...), custom_call_target="tpu_custom_call" | custom-call | flops 14495514624 | bytes 47185920 | tf_op jit(solution)/shard_map/block/pallas_call | solution.py:1511
  92.0 60.0 %tail.1 = (bf16[16,192,256]{2,1,0:T(8,128)(2,1)}, bf16[2,16,192,256]{3,2,1,0:T(8,128)(2,1)}, f32[2,384]{1,0:T(2,128)}, bf16[7,2,4,48,384]{4,3,2,1,0:T(8,128)(2,1)}) custom-call(s32[32]{0:T(128)} %refs_0_.3, f32[16,128,768]{2,1,0:T(8,128)} %get-tuple-element.45.dz2, f32[2,16,768]{2,1,0:T(8,128)} %get-tuple-element.46.dzland, ...), custom_call_target="tpu_custom_call" | custom-call | flops 13287555072 | bytes 62914560 | tf_op jit(solution)/shard_map/tail/pallas_call | solution.py:1592
  152.0 10.6 %input_grad.1 = (bf16[32,192,256]{2,1,0:T(8,128)(2,1)}, bf16[32,192,128]{2,1,0:T(8,128)(2,1)}, f32[5,192,768]{2,1,0:T(8,128)}, f32[3,96,768]{2,1,0:T(8,128)}, f3...) custom-call(s32[32]{0:T(128)} %refs_0_.3, ...), custom_call_target="tpu_custom_call" | custom-call | flops 1207959552 | bytes 12582912 | tf_op jit(solution)/shard_map/input_grad/pallas_call | solution.py:1655
